TPU v7x, 512 devices: a whole 4x8x8 slice. The times are simulated.
512 devices in a mesh: dp: 64 (over z_hi, y, core), tensor: 8 (over x, z_lo).
Axes of the slice: x: 4, y: 8, z: 8 (z_hi: 4, z_lo: 2; z = z_hi * 2 + z_lo), core: 2. Of those that a mesh axis runs over, the one named last changes fastest.
Arguments:
- teacher: bfloat16 [16384, 3072], P('dp', 'tensor'), may hold values from -6 to 6
- projector: bfloat16 [3072, 2048], P('tensor', 'dp'), may hold values from -0.109375 to 0.109375
- residual: bfloat16 [16384, 2048], P(('dp', 'tensor')), may hold values from -6 to 6
- gate_pre: bfloat16 [16384, 8192], P('dp', 'tensor'), may hold values from -6 to 6
- up_pre: bfloat16 [16384, 8192], P('dp', 'tensor'), may hold values from -6 to 6
- down_weight: bfloat16 [8192, 2048], P('tensor', 'dp'), may hold values from -0.0625 to 0.0625
Outputs:
- projector_grad: float32 [3072, 2048], P('tensor', 'dp')
- grad_residual: bfloat16 [16384, 2048], P(('dp', 'tensor'))
- grad_gate: bfloat16 [16384, 8192], P('dp', 'tensor')
- grad_up: bfloat16 [16384, 8192], P('dp', 'tensor')
All inputs are finite; a program needn't handle non-finite values.
Results may differ from a plain program's by a relative error of at most 0.015.
Values may be sent and summed in bfloat16 or wider, within the bound.
A program may use at most 64 MiB of HBM per device.

v0:
```python
import math

import jax
import jax.numpy as jnp
from jax import lax
from jax.sharding import PartitionSpec as P


def per_device(teacher, projector, residual, gate_pre, up_pre, down_weight):
    group_rows = teacher.shape[0]
    ways = lax.axis_size("tensor")
    share = group_rows // ways
    token_total = group_rows * lax.axis_size("dp")
    gate = gate_pre.astype(jnp.float32)
    upper = up_pre.astype(jnp.float32)
    sig = jax.nn.sigmoid(gate)
    hidden = (gate * sig * upper).astype(jnp.bfloat16)
    projected = jnp.dot(
        teacher,
        lax.all_gather(projector, "dp", axis=1, tiled=True),
        preferred_element_type=jnp.float32,
    )
    down_whole = lax.all_gather(down_weight, "dp", axis=1, tiled=True)
    mlp_term = jnp.dot(hidden, down_whole, preferred_element_type=jnp.float32)
    parts = mlp_term - projected
    stacked = parts.astype(jnp.bfloat16).reshape(ways, share, parts.shape[1])
    received = lax.all_to_all(stacked, "tensor", split_axis=0, concat_axis=0, tiled=True)
    summed = jnp.sum(received.astype(jnp.float32), axis=0)
    grad_own = (residual.astype(jnp.float32) + summed).astype(jnp.bfloat16)
    grad_rows = lax.all_gather(grad_own, "tensor", axis=0, tiled=True)
    contract_cols = (((1,), (1,)), ((), ()))
    hidden_grad = lax.dot_general(
        grad_rows, down_whole, contract_cols, preferred_element_type=jnp.float32
    )
    grad_up = (hidden_grad * gate * sig).astype(jnp.bfloat16)
    grad_gate = (hidden_grad * upper * sig * (1.0 + gate * (1.0 - sig))).astype(jnp.bfloat16)
    local_grad = lax.dot_general(
        teacher, grad_rows, (((0,), (0,)), ((), ())), preferred_element_type=jnp.float32
    )
    projector_grad = lax.psum_scatter(
        local_grad, "dp", scatter_dimension=1, tiled=True
    ) / math.sqrt(token_total)
    return (projector_grad, grad_own, grad_gate, grad_up)


def solution(mesh):
    in_specs = (
        P("dp", "tensor"),
        P("tensor", "dp"),
        P(("dp", "tensor"), None),
        P("dp", "tensor"),
        P("dp", "tensor"),
        P("tensor", "dp"),
    )
    out_specs = (P("tensor", "dp"), P(("dp", "tensor"), None), P("dp", "tensor"), P("dp", "tensor"))
    return jax.shard_map(
        per_device, mesh=mesh, in_specs=in_specs, out_specs=out_specs, check_vma=False
    )
```

profile of v0, /device:TPU:1, one launch (start us, length us, event | category | flops | bytes accessed | tf_op | source)
XLA Modules:
  0.0 413.7 jit_solution(8088165536229022003)
XLA Ops:
  7.2 0.0 copy-start
  7.2 0.0 all-gather.4.cloned.1.call-start
  7.2 0.7 all-gather.4.cloned.1.call-update
  7.9 0.0 all-gather.6.cloned.1.call-start
  8.0 0.7 all-gather.6.cloned.1.call-update
  8.7 0.0 all-gather.8.cloned.1.call-start
  8.7 97.0 %all-gather.4.cloned.1.call-done = bf16[1024,2048]{0,1:T(8,128)(2,1)} async-done(((bf16[1024,32]{0,1:T(8,128)(2,1)}), bf16[1024,2048]{0,1:T(8,128)(2,1)}) %all-gather.4.cloned.1.call-update) | async-done | bytes 4194320 | tf_op jit(solution)/shard_map/all_gather | solution.py:23
  105.7 3.9 fusion.11
  109.6 79.1 %all-gather.6.cloned.1.call-done = bf16[384,2048]{0,1:T(8,128)(2,1)} async-done(((bf16[384,32]{0,1:T(8,128)(2,1)}), bf16[384,2048]{0,1:T(8,128)(2,1)}) %all-gather.6.cloned.1.call-update) | async-done | bytes 1572880 | tf_op jit(solution)/shard_map/all_gather | solution.py:20
  188.6 0.0 copy-done
  188.6 2.1 fusion
  190.8 0.0 copy-start.2
  190.8 19.0 %all_to_all.5 = bf16[8,32,2048]{2,1,0:T(8,128)(2,1)S(1)} all-to-all(bf16[8,32,2048]{2,1,0:T(8,128)(2,1)S(1)} %bitcast.10), channel_id=1, replica_groups=mesh['dp'=64,'tensor'=8] {'tensor'}, dimensions={0} | all-to-all | bytes 2097152 | tf_op jit(solution)/shard_map/all_to_all | solution.py:27
  209.8 0.1 convert_reduce_fusion
  209.9 0.0 copy-done.2
  209.9 0.7 add_convert_fusion
  210.6 0.0 all-gather.8.cloned.1.call-update
  210.6 0.0 reduce-scatter.2.cloned.1.call-start
  210.7 37.4 %all-gather.8.cloned.1.call-done = bf16[256,2048]{1,0:T(8,128)(2,1)} async-done(((bf16[32,2048]{1,0:T(8,128)(2,1)}), bf16[256,2048]{1,0:T(8,128)(2,1)}) %all-gather.8.cloned.1.call-update) | async-done | bytes 1048592 | tf_op jit(solution)/shard_map/all_gather | solution.py:30
  248.1 3.7 convolution_bitcast_fusion
  251.7 0.0 copy-start.1
  251.7 0.0 copy-start.3
  251.7 0.0 copy-start.4
  251.7 0.0 reduce-scatter.2.cloned.1.call-update
  251.8 1.2 copy-done.1
  253.0 0.1 copy-done.3
  253.1 0.2 copy-done.4
  253.3 4.7 %fusion.10 = (bf16[256,1024]{1,0:T(8,128)(2,1)}, bf16[256,1024]{1,0:T(8,128)(2,1)}) fusion(bf16[256,1024]{1,0:T(8,128)(2,1)S(1)} %copy-done.4, bf16[256,1024]{1,0:T(8,128)(2,1)S(1)} %copy-done.3, bf16[256,2048]{1,0:T(8,128)(2,1)S(1)} %copy-done.1, bf16[1024,2048]{0,1:T(8,128)(2,1)} %all-gather.4.cloned.1.call-done), kind=kOutput, calls=%fused_computation.19 | convolution fusion | flops 1077673984 | bytes 7340032 | tf_op jit(solution)/shard_map/dot_general | solution.py:32
  258.0 147.8 %reduce-scatter.2.cloned.1.call-done = f32[384,32]{0,1:T(8,128)} async-done(((f32[384,2048]{0,1:T(8,128)}), f32[384,32]{0,1:T(8,128)}) %reduce-scatter.2.cloned.1.call-update) | async-done | bytes 49168 | tf_op jit(solution)/shard_map/reduce_scatter | solution.py:40
  405.7 1.4 broadcast_multiply_fusion
Async XLA Ops:
  7.2 181.5 %copy-start = (bf16[256,384]{1,0:T(8,128)(2,1)S(1)}, bf16[256,384]{1,0:T(8,128)(2,1)}, u32[]{:S(2)}) copy-start(bf16[256,384]{1,0:T(8,128)(2,1)} %param.6) | copy-start | bytes 589828
  7.2 98.5 %all-gather.4.cloned.1.call-start = ((), (), s32[]{:S(2)}) async-start(), calls=%async_computation.2 | async-start | bytes 4259840 | tf_op jit(solution)/shard_map/all_gather | solution.py:23
  7.9 180.7 %all-gather.6.cloned.1.call-start = ((), (), s32[]{:S(2)}) async-start(), calls=%async_computation.3 | async-start | bytes 1597440 | tf_op jit(solution)/shard_map/all_gather | solution.py:20
  8.7 239.4 %all-gather.8.cloned.1.call-start = ((), (), s32[]{:S(2)}) async-start(), calls=%async_computation.4 | async-start | bytes 1179648 | tf_op jit(solution)/shard_map/all_gather | solution.py:30
  190.8 19.2 %copy-start.2 = (bf16[32,2048]{1,0:T(8,128)(2,1)S(1)}, bf16[32,2048]{1,0:T(8,128)(2,1)}, u32[]{:S(2)}) copy-start(bf16[32,2048]{1,0:T(8,128)(2,1)} %param.8) | copy-start | bytes 393220
  210.6 195.1 %reduce-scatter.2.cloned.1.call-start = ((), (), s32[]{:S(2)}) async-start(), calls=%async_computation.5 | async-start | bytes 3194880 | tf_op jit(solution)/shard_map/reduce_scatter | solution.py:40
  251.7 1.2 copy-start.1
  251.7 1.4 copy-start.3
  251.7 1.5 copy-start.4
Sparse Core Ops, SparseCore 0:
  11.4 94.2 all-gather.3
  109.0 79.6 all-gather.5
  210.8 37.2 all-gather.7
  252.6 153.0 reduce-scatter.1
where the time goes:
time: 418 us; the launch traced here: 414 us
  waiting for transfers between devices  363 us (87%)
  blocking collectives  19 us (5%)
  matrix products  14.4 us (3%)
  between operations  13.8 us (3%)
    reduce_scatter x1, waiting for transfers between devices, per_device(): lax.psum_scatter(local_grad, 'dp', scatter_dimension=1, tiled=True)  148 us
    all_gather x1, waiting for transfers between devices, per_device(): down_whole = lax.all_gather(down_weight, 'dp', axis=1, tiled=True)  97 us
    all_gather x1, waiting for transfers between devices, per_device(): lax.all_gather(projector, 'dp', axis=1, tiled=True)  79.1 us
    all_gather x1, waiting for transfers between devices, per_device(): grad_rows = lax.all_gather(grad_own, 'tensor', axis=0, tiled=True)  37.4 us
    all_to_all x1, blocking collectives, per_device(): lax.all_to_all(stacked, 'tensor', split_axis=0, concat_axis=0, tiled=True)  19 us
  transfers between devices with their start and end apart: 4, of which 4 were waited for; matrix products, arithmetic and copies ran while one was open for 2% of the time, Pallas kernels for 0%

commit v1 on v0

v1 whole, which is shorter than its diff:
```python
import math

import jax
import jax.numpy as jnp
from jax import lax
from jax.experimental import pallas as pl
from jax.experimental.pallas import tpu as pltpu
from jax.sharding import PartitionSpec as P

NY, NZ, NT = 8, 4, 8
MESH = pl.DeviceIdType.MESH
F32, BF16 = jnp.float32, jnp.bfloat16
GRAY = (0, 1, 3, 2)


def kernel(
    w_in, p_in, teacher, residual, gate, up,
    pg_out, gr_out, gg_out, gu_out,
    wall, hid, parts, rbuf, rows, hgrad, lgf, lgb, lgr, ysend, yland, zsend, zland,
    bz_s, bz_r, wz_s, wz_r, wy_s, wy_r, ws_s, ws_r, ex_s, ex_r, ag_s, ag_r,
    ls_s, ls_r, ry_s, ry_r,
):
    dp = lax.axis_index("dp")
    me = lax.axis_index("tensor")
    c = lax.rem(dp, 2)
    y = lax.rem(lax.div(dp, 2), NY)
    zh = lax.div(dp, 2 * NY)

    def dev(cc, yy, zz, tt):
        return ((zz * NY + yy) * 2 + cc, tt)

    def ymod(s):
        return lax.rem(y + s + NY, NY)

    def zmod(s):
        return lax.rem(zh + s + NZ, NZ)

    sib = dev(1 - c, y, zh, me)
    up_y = dev(c, ymod(1), zh, me)
    dn_y = dev(c, ymod(-1), zh, me)

    def zdev(q):
        return dev(c, y, zmod(q), me)

    def tdev(d):
        return (dp, lax.rem(me + d, NT))

    def rc(src, dst, ssem, rsem, to):
        return pltpu.make_async_remote_copy(
            src_ref=src, dst_ref=dst, send_sem=ssem, recv_sem=rsem,
            device_id=to, device_id_type=MESH,
        )

    def loc(yy, zz, cc):
        return wall.at[lax.div(yy, 2), zz, lax.rem(yy, 2), cc]

    k0 = lax.div(y, 2)
    par = lax.rem(y, 2)
    wall[k0, zh, par, c, :, :1024] = w_in[...]
    wall[k0, zh, par, c, :, 1024:] = p_in[...]

    barrier = pltpu.get_barrier_semaphore()
    peers = [sib, up_y, dn_y] + [zdev(q) for q in (1, 2, 3)] + [tdev(d) for d in range(1, NT)]
    for to in peers:
        pl.semaphore_signal(barrier, inc=1, device_id=to, device_id_type=MESH)
    pl.semaphore_wait(barrier, len(peers))

    def wz(q):
        u = loc(y, zh, c)
        return rc(u, u, wz_s.at[q - 1], wz_r.at[q - 1], zdev(q))

    def wz_in(q):
        u = loc(y, zmod(-q), c)
        return rc(u, u, wz_s.at[q - 1], wz_r.at[q - 1], zdev(q))

    def wy(d, s, j):
        sign = 1 - 2 * d
        u = loc(ymod(-sign * (s - 1)), zmod(-j), c)
        return rc(u, u, wy_s.at[d, s - 1, j], wy_r.at[d, s - 1, j], (up_y, dn_y)[d])

    def wy_in(d, s, j):
        sign = 1 - 2 * d
        u = loc(ymod(-sign * s), zmod(-j), c)
        return rc(u, u, wy_s.at[d, s - 1, j], wy_r.at[d, s - 1, j], (up_y, dn_y)[d])

    def ws(d, s, j, cc):
        sign = 1 - 2 * d
        u = loc(ymod(-sign * s), zmod(-j), cc)
        return rc(u, u, ws_s.at[d, s, j], ws_r.at[d, s, j], sib)

    def share(d, s, j):
        ws(d, s, j, c).start()

    for q in (1, 3, 2):
        wz(q).start()
    for d in (0, 1):
        wy(d, 1, 0).start()
    share(0, 0, 0)

    @pl.loop(0, 8)
    def _(r):
        at = pl.ds(pl.multiple_of(r * 32, 32), 32)
        g = gate[at, :].astype(F32)
        u = up[at, :].astype(F32)
        hid[at, :1024] = (g * jax.nn.sigmoid(g) * u).astype(BF16)
        hid[at, 1024:] = -teacher[at, :]

    for q in (1, 3, 2):
        wz_in(q).wait_recv()
        for d in (0, 1):
            wy(d, 1, q).start()
        share(0, 0, q)

    def y_unit(s, n):
        j = GRAY[n]
        for d in (0, 1):
            if s == 4 and (n >= 2) != (d == 1):
                continue
            wy_in(d, s, j).wait_recv()
            if s < 3 or (s == 3 and (n >= 2) == (d == 1)):
                wy(d, s + 1, j).start()
            share(d, s, j)

    def sib_wait(s):
        for n in range(4):
            j = GRAY[n]
            if s == 0:
                ws(0, 0, j, 1 - c).wait_recv()
                continue
            for d in (0, 1):
                if s == 4 and (n >= 2) != (d == 1):
                    continue
                ws(d, s, j, 1 - c).wait_recv()

    turn = 2 * par - 1
    pair = [k0, lax.rem(k0 + turn + 4, 4), lax.rem(k0 - turn + 4, 4), lax.rem(k0 + 2, 4)]

    def span(i, z):
        return pl.ds(pl.multiple_of(z * 512 + pair[i] * 128, 128), 128)

    def ex(i, d):
        give = pl.ds(pl.multiple_of(lax.rem(me + d, NT) * 32, 32), 32)
        return rc(parts.at[i, give, :], rbuf.at[i, d - 1], ex_s.at[i, d - 1], ex_r.at[i, d - 1], tdev(d))

    mine = pl.ds(pl.multiple_of(me * 32, 32), 32)

    def ag(i, d):
        return rc(rows.at[i, mine, :], rows.at[i, mine, :], ag_s.at[i, d - 1], ag_r.at[i, d - 1], tdev(d))

    def ag_in(i, d):
        at = pl.ds(pl.multiple_of(lax.rem(me - d + NT, NT) * 32, 32), 32)
        return rc(rows.at[i, at, :], rows.at[i, at, :], ag_s.at[i, d - 1], ag_r.at[i, d - 1], tdev(d))

    def stage_a(i):
        w = wall[pair[i]].reshape(512, 1408)
        out = lax.dot_general(hid[...], w, (((1,), (1,)), ((), ())), preferred_element_type=F32)
        parts[i] = out.astype(BF16)
        for d in range(1, NT):
            ex(i, d).start()

    def stage_b(i):
        acc = parts[i, mine, :].astype(F32)
        for d in range(1, NT):
            ex(i, d).wait_recv()
            acc = acc + rbuf[i, d - 1].astype(F32)
        for z in range(4):
            at = span(i, z)
            g = (residual[:, at].astype(F32) + acc[:, z * 128:(z + 1) * 128]).astype(BF16)
            gr_out[:, at] = g
            rows[i, mine, z * 128:(z + 1) * 128] = g
        for d in range(1, NT):
            ag(i, d).start()

    def ls(i):
        return rc(lgb.at[pair[i], :, :, 1 - c], lgr.at[pair[i]], ls_s.at[i], ls_r.at[i], sib)

    def stage_c(i):
        for d in range(1, NT):
            ag_in(i, d).wait_recv()
        g = rows[i]
        lg = lax.dot_general(g, teacher[...], (((0,), (0,)), ((), ())), preferred_element_type=F32)
        lg = lg.reshape(4, 2, 2, 32, 384)
        lgf[pair[i]] = lg
        lgb[pair[i]] = lg.astype(BF16)
        ls(i).start()
        w = wall[pair[i], :, :, :, :, :1024].reshape(512, 1024)
        h = jnp.dot(g, w, preferred_element_type=F32)
        if i == 0:
            hgrad[...] = h
        else:
            hgrad[...] += h

    sib_wait(0)
    for n in range(4):
        y_unit(1, n)
    sib_wait(1)
    stage_a(0)
    for s in (2, 3, 4):
        y_unit(s, 0)
        y_unit(s, 1)
        stage_b(s - 2)
        y_unit(s, 2)
        y_unit(s, 3)
        sib_wait(s)
        stage_a(s - 1)
        stage_c(s - 2)
    stage_b(3)
    stage_c(3)

    for i in range(4):
        ls(i).wait_recv()

    def own(yy, zs):
        k, p = lax.div(yy, 2), lax.rem(yy, 2)
        return lgf[k, zs:zs + 2, p, c] + lgr[k, zs:zs + 2, p].astype(F32)

    def ry(d, s, h):
        return rc(ysend.at[d, s - 1, h], yland.at[d, s - 1, h], ry_s.at[d, s - 1, h], ry_r.at[d, s - 1, h], (up_y, dn_y)[d])

    def ring(s):
        for h in (0, 1):
            for d in (0, 1):
                if s == 1 and h != d:
                    continue
                sign = 1 - 2 * d
                t = own(ymod(sign * (5 - s)), 2 * h)
                if s > 2 or (s == 2 and h == d):
                    ry(d, s - 1, h).wait_recv()
                    t = t + yland[d, s - 2, h].astype(F32)
                ysend[d, s - 1, h] = t.astype(BF16)
                ry(d, s, h).start()

    def backward(r0, r1):
        @pl.loop(r0, r1)
        def _(r):
            at = pl.ds(pl.multiple_of(r * 32, 32), 32)
            g = gate[at, :].astype(F32)
            u = up[at, :].astype(F32)
            hg = hgrad[at, :]
            sig = jax.nn.sigmoid(g)
            gu_out[at, :] = (hg * g * sig).astype(BF16)
            gg_out[at, :] = (hg * u * sig * (1.0 + g * (1.0 - sig))).astype(BF16)

    for s in (1, 2, 3, 4):
        ring(s)
        backward(2 * s - 2, 2 * s)

    for h in (0, 1):
        t = own(y, 2 * h)
        for d in (0, 1):
            ry(d, 4, h).wait_recv()
            t = t + yland[d, 3, h].astype(F32)
        zsend[2 * h:2 * h + 2] = t
    for z in range(4):
        zland[3, z] = zsend[z].astype(BF16)

    def rz(q):
        return rc(zland.at[3, zmod(q)], zland.at[q - 1, 0], bz_s.at[q - 1], bz_r.at[q - 1], zdev(q))

    for q in (1, 3, 2):
        rz(q).start()
    t = zsend[zh]
    for q in (1, 3, 2):
        rz(q).wait_recv()
        t = t + zland[q - 1, 0].astype(F32)
    pg_out[...] = t * (1.0 / 128.0)

    for q in (1, 2, 3):
        wz(q).wait_send()
        rz(q).wait_send()
    for d in (0, 1):
        for n in range(4):
            j = GRAY[n]
            for s in range(0, 5):
                if s == 0 and d == 1:
                    continue
                if s == 4 and (n >= 2) != (d == 1):
                    continue
                ws(d, s, j, c).wait_send()
                if s > 0:
                    wy(d, s, j).wait_send()
        for h in (0, 1):
            for s in range(1, 5):
                if s == 1 and h != d:
                    continue
                ry(d, s, h).wait_send()
    for i in range(4):
        ls(i).wait_send()
        for d in range(1, NT):
            ex(i, d).wait_send()
            ag(i, d).wait_send()


def per_device(teacher, projector, residual, gate_pre, up_pre, down_weight):
    vm = pl.BlockSpec(memory_space=pltpu.VMEM)
    dma = pltpu.SemaphoreType.DMA
    pg, gr, gg, gu = pl.pallas_call(
        kernel,
        out_shape=(
            jax.ShapeDtypeStruct((32, 384), F32),
            jax.ShapeDtypeStruct((32, 2048), BF16),
            jax.ShapeDtypeStruct((256, 1024), BF16),
            jax.ShapeDtypeStruct((256, 1024), BF16),
        ),
        in_specs=[vm] * 6,
        out_specs=(vm,) * 4,
        scratch_shapes=[
            pltpu.VMEM((4, 4, 2, 2, 32, 1408), BF16),
            pltpu.VMEM((256, 1408), BF16),
            pltpu.VMEM((4, 256, 512), BF16),
            pltpu.VMEM((4, 7, 32, 512), BF16),
            pltpu.VMEM((4, 256, 512), BF16),
            pltpu.VMEM((256, 1024), F32),
            pltpu.VMEM((4, 4, 2, 2, 32, 384), F32),
            pltpu.VMEM((4, 4, 2, 2, 32, 384), BF16),
            pltpu.VMEM((4, 4, 2, 32, 384), BF16),
            pltpu.VMEM((2, 4, 2, 2, 32, 384), BF16),
            pltpu.VMEM((2, 4, 2, 2, 32, 384), BF16),
            pltpu.VMEM((4, 32, 384), F32),
            pltpu.VMEM((4, 4, 32, 384), BF16),
            dma((3,)), dma((3,)), dma((3,)), dma((3,)),
            dma((2, 4, 4)), dma((2, 4, 4)), dma((2, 5, 4)), dma((2, 5, 4)),
            dma((4, 7)), dma((4, 7)), dma((4, 7)), dma((4, 7)),
            dma((4,)), dma((4,)), dma((2, 4, 2)), dma((2, 4, 2)),
        ],
        compiler_params=pltpu.CompilerParams(
            collective_id=0, has_side_effects=True, vmem_limit_bytes=56 * 1024 * 1024
        ),
        cost_estimate=pl.CostEstimate(flops=2950000000, bytes_accessed=4000000, transcendentals=524288),
    )(down_weight.T, projector.T, teacher, residual, gate_pre, up_pre)
    return pg.T, gr, gg, gu


def solution(mesh):
    in_specs = (
        P("dp", "tensor"),
        P("tensor", "dp"),
        P(("dp", "tensor"), None),
        P("dp", "tensor"),
        P("dp", "tensor"),
        P("tensor", "dp"),
    )
    out_specs = (P("tensor", "dp"), P(("dp", "tensor"), None), P("dp", "tensor"), P("dp", "tensor"))
    return jax.shard_map(
        per_device, mesh=mesh, in_specs=in_specs, out_specs=out_specs, check_vma=False
    )
```

time: 418 us -> 102 us (0.24)
  the two profiles are of different devices: /device:TPU:1 before, /device:TPU:8 now
where the time goes in v1:
time: 102 us
  Pallas kernels  95.8 us (94%)
  local copies, waits for them, and re-layouts  5.71 us (6%)
    pallas_call x1, Pallas kernels, per_device(): pl.pallas_call(kernel, out_shape=(jax.ShapeDtypeStruct((32, 384), F32), j...  95.8 us
    unnamed x6, local copies, waits for them, and re-layouts  5.71 us

profile of v1, /device:TPU:8, one launch (start us, length us, event | category | flops | bytes accessed | tf_op | source)
XLA Modules:
  0.0 102.1 jit_solution(2967009202148749251)
XLA Ops:
  0.6 95.8 %shard_map.93 = (f32[32,384]{1,0:T(8,128)}, bf16[32,2048]{1,0:T(8,128)(2,1)}, bf16[256,1024]{1,0:T(8,128)(2,1)}, bf16[256,1024]{1,0:T(8,128)(2,1)}) custom-call(bf16[32,1024]{1,0:T(8,128)(2,1)} %bitcast.4, bf16[32,384]{1,0:T(8,128)(2,1)} %bitcast.5, bf16[256,384]{1,0:T(8,128)(2,1)} %teacher.1, bf16[32,2048]{1,0:T(8,128)(2,1)} %residual.1, ...), custom_call_target="tpu_custom_call" | custom-call | flops 2950000128 | bytes 4000000 | tf_op jit(solution)/shard_map/pallas_call | solution.py:297
  96.4 1.4 %copy.14 = f32[384,32]{0,1:T(8,128)} copy(f32[384,32]{0,1:T(8,128)} %bitcast.3) | data formatting | bytes 98304
  97.8 1.6 %copy.15 = bf16[32,2048]{1,0:T(8,128)(2,1)} copy(bf16[32,2048]{1,0:T(8,128)(2,1)} %get-tuple-element.17) | data formatting | bytes 262144
  99.4 0.0 copy-start
  99.4 1.9 %copy.16 = bf16[256,1024]{1,0:T(8,128)(2,1)} copy(bf16[256,1024]{1,0:T(8,128)(2,1)} %get-tuple-element.18) | data formatting | bytes 1048576
  101.3 0.0 copy-done
  101.3 0.8 copy.17
Async XLA Ops:
  99.4 1.9 %copy-start = (bf16[256,1024]{1,0:T(8,128)(2,1)S(1)}, bf16[256,1024]{1,0:T(8,128)(2,1)}, u32[]{:S(2)}) copy-start(bf16[256,1024]{1,0:T(8,128)(2,1)} %get-tuple-element.19) | copy-start | bytes 1572868

commit v2 on v0

v2 whole, which is shorter than its diff:
```python
import math

import jax
import jax.numpy as jnp
from jax import lax
from jax.experimental import pallas as pl
from jax.experimental.pallas import tpu as pltpu
from jax.sharding import PartitionSpec as P

NY, NZ, NT = 8, 4, 8
MESH = pl.DeviceIdType.MESH
F32, BF16 = jnp.float32, jnp.bfloat16
CHUNKS = (
    ((0, 0),),
    ((0, 1),),
    ((1, 0), (3, 0)),
    ((0, 2), (1, 1), (3, 1)),
    ((2, 0), (0, 3)),
    ((2, 1), (1, 2), (3, 2)),
    ((1, 3), (3, 3), (2, 2)),
    ((2, 3),),
)
NC = len(CHUNKS)
WIDE = 128 * max(len(ch) for ch in CHUNKS)
YORD = (4, 3, 5, 2, 6, 1, 7)


def kernel(
    w_in, p_in, teacher_in, residual_in, gate_in, up_in,
    pg_out, gr_out, gg_out, gu_out,
    teacher, residual, gate, up,
    wall, hid, parts, rbuf, rows, hgrad, lgf, lgb, lgr, acc0, ysend, yland, zsend, zland, fsend, fland,
    in_s, wz_s, wz_r, wy_s, wy_r, ws_s, ws_r, ex_s, ex_r, ag_s, ag_r,
    ls_s, ls_r, ry_s, ry_r, rz_s, rz_r, rf_s, rf_r,
):
    dp = lax.axis_index("dp")
    me = lax.axis_index("tensor")
    c = lax.rem(dp, 2)
    y = lax.rem(lax.div(dp, 2), NY)
    zh = lax.div(dp, 2 * NY)

    def dev(cc, yy, zz, tt):
        return ((zz * NY + yy) * 2 + cc, tt)

    def ymod(s):
        return lax.rem(y + s + NY, NY)

    def zmod(s):
        return lax.rem(zh + s + NZ, NZ)

    sib = dev(1 - c, y, zh, me)
    ydev = (dev(c, ymod(1), zh, me), dev(c, ymod(-1), zh, me))

    def zdev(q):
        return dev(c, y, zmod(q), me)

    def tdev(d):
        return (dp, lax.rem(me + d, NT))

    barrier = pltpu.get_barrier_semaphore()
    peers = [sib] + [dev(c, ymod(d), zh, me) for d in range(1, NY)] + [zdev(q) for q in (1, 2, 3)] + [tdev(d) for d in range(1, NT)]
    for to in peers:
        pl.semaphore_signal(barrier, inc=1, device_id=to, device_id_type=MESH)

    loads = [
        pltpu.make_async_copy(w_in, wall.at[zh, y, c, :, 0:1024], in_s.at[0]),
        pltpu.make_async_copy(p_in, wall.at[zh, y, c, :, 1024:1408], in_s.at[1]),
        pltpu.make_async_copy(gate_in, gate, in_s.at[2]),
        pltpu.make_async_copy(up_in, up, in_s.at[3]),
        pltpu.make_async_copy(teacher_in, teacher, in_s.at[4]),
        pltpu.make_async_copy(residual_in, residual, in_s.at[5]),
    ]
    for load in loads:
        load.start()
    loads[0].wait()
    loads[1].wait()
    pl.semaphore_wait(barrier, len(peers))

    pend = {}

    def go(key, send, recv):
        send.start()
        pend[key] = [send, recv, False]

    def got(key):
        pend[key][1].wait_recv()
        pend[key][2] = True

    def drain():
        for send, recv, done in pend.values():
            if not done:
                recv.wait_recv()
        for send, recv, done in pend.values():
            send.wait_send()

    def rc(src, dst, ssem, rsem, to):
        return pltpu.make_async_remote_copy(
            src_ref=src, dst_ref=dst, send_sem=ssem, recv_sem=rsem,
            device_id=to, device_id_type=MESH,
        )

    def half(u, d):
        return u.at[16 * d:16 * d + 16, :]

    def copy_z(q):
        def at(z):
            u = wall.at[z, y, c]
            return rc(u, u, wz_s.at[q], wz_r.at[q], zdev(q))
        go(("wz", q), at(zh), at(zmod(-q)))

    def relay_z(d):
        def at(z):
            u = half(wall.at[z, y, c], d)
            return rc(u, u, wz_s.at[2 * d], wz_r.at[2 * d], zdev((1, -1)[d]))
        go(("wz2", d), at(zmod((-1, 1)[d])), at(zmod(2)))

    def copy_y(d, s, j):
        sign = 1 - 2 * d

        def at(yy):
            u = wall.at[zmod(-j), yy, c]
            if s == 4:
                u = half(u, d)
            return rc(u, u, wy_s.at[d, s - 1, j], wy_r.at[d, s - 1, j], ydev[d])
        go(("wy", d, s, j), at(ymod(-sign * (s - 1))), at(ymod(-sign * s)))

    def share(d, s, j):
        sign = 1 - 2 * d

        def at(cc):
            u = wall.at[zmod(-j), ymod(-sign * s), cc]
            if s == 4:
                u = half(u, d)
            return rc(u, u, ws_s.at[d, s, j], ws_r.at[d, s, j], sib)
        go(("ws", d, s, j), at(c), at(1 - c))

    def first(j):
        for d in (0, 1):
            copy_y(d, 1, j)
        share(0, 0, j)

    def unit(s, j):
        for d in (0, 1):
            got(("wy", d, s, j))
            if s < 4:
                copy_y(d, s + 1, j)
            share(d, s, j)

    def need(j, last):
        for s in range(last + 1):
            for d in (0, 1):
                if (s > 0 or d == 0) and not pend[("ws", d, s, j)][2]:
                    got(("ws", d, s, j))

    def make_hidden():
        for load in loads[2:5]:
            load.wait()

        @pl.loop(0, 8)
        def _(r):
            at = pl.ds(pl.multiple_of(r * 32, 32), 32)
            g = gate[at, :].astype(F32)
            u = up[at, :].astype(F32)
            hid[at, :1024] = (g * jax.nn.sigmoid(g) * u).astype(BF16)
            hid[at, 1024:] = -teacher[at, :]

    mine = pl.ds(pl.multiple_of(me * 32, 32), 32)
    k0 = lax.div(y, 2)
    turn = 2 * lax.rem(y, 2) - 1
    pair = (k0, lax.rem(k0 + turn + 4, 4), lax.rem(k0 - turn + 4, 4), lax.rem(k0 + 2, 4))

    def two(p):
        return pl.ds(2 * pair[p], 2)

    def cut(i):
        return slice(128 * i, 128 * i + 128)

    def stage_a(n):
        w = 128 * len(CHUNKS[n])
        for i, (j, p) in enumerate(CHUNKS[n]):
            need(j, p + 1)
            wt = wall[zmod(-j), two(p)].reshape(128, 1408)
            out = lax.dot_general(hid[...], wt, (((1,), (1,)), ((), ())), preferred_element_type=F32)
            parts[n, :, cut(i)] = out.astype(BF16)
        for d in YORD:
            give = pl.ds(pl.multiple_of(lax.rem(me + d, NT) * 32, 32), 32)
            copy = rc(
                parts.at[n, give, 0:w], rbuf.at[n, d - 1, :, 0:w],
                ex_s.at[n, d - 1], ex_r.at[n, d - 1], tdev(d),
            )
            go(("ex", n, d), copy, copy)

    def stage_b(n):
        w = 128 * len(CHUNKS[n])
        acc = parts[n, mine, 0:w].astype(F32)
        for d in YORD:
            got(("ex", n, d))
            acc = acc + rbuf[n, d - 1, :, 0:w].astype(F32)
        for i, (j, p) in enumerate(CHUNKS[n]):
            cols = pl.ds(pl.multiple_of(zmod(-j) * 512 + pair[p] * 128, 128), 128)
            g = (acc[:, cut(i)] + residual[:, cols].astype(F32)).astype(BF16)
            gr_out[:, cols] = g
            rows[n, mine, cut(i)] = g

        def copy(d, who):
            r = rows.at[n, pl.ds(pl.multiple_of(who * 32, 32), 32), 0:w]
            return rc(r, r, ag_s.at[n, d - 1], ag_r.at[n, d - 1], tdev(d))
        for d in YORD:
            go(("ag", n, d), copy(d, me), copy(d, lax.rem(me - d + NT, NT)))

    def stage_c(n):
        for d in YORD:
            got(("ag", n, d))
        for i, (j, p) in enumerate(CHUNKS[n]):
            lg = lax.dot_general(
                rows[n, :, cut(i)], teacher[...], (((0,), (0,)), ((), ())), preferred_element_type=F32
            ).reshape(2, 2, 32, 384)
            lgf[j, two(p)] = lg
            lgb[j, two(p)] = lg.astype(BF16)
            copy = rc(
                lgb.at[j, two(p), 1 - c], lgr.at[j, two(p)], ls_s.at[j, p], ls_r.at[j, p], sib,
            )
            go(("ls", j, p), copy, copy)

    def stage_h(n):
        h = None
        for i, (j, p) in enumerate(CHUNKS[n]):
            wt = wall[zmod(-j), two(p), :, :, :1024].reshape(128, 1024)
            one = jnp.dot(rows[n, :, cut(i)], wt, preferred_element_type=F32)
            h = one if h is None else h + one
        if n == 0:
            hgrad[...] = h
        else:
            hgrad[...] += h

    def paired(n):
        for j, p in CHUNKS[n]:
            got(("ls", j, p))
            if j == 2:
                continue
            t = lgf[j, two(p), c] + lgr[j, two(p)].astype(F32)
            if j == 0:
                acc0[two(p)] = t
            else:
                q = j // 2
                zsend[q, two(p)] = t.astype(BF16)
                copy = rc(
                    zsend.at[q, two(p)], zland.at[q, two(p)], rz_s.at[q, p], rz_r.at[q, p], zdev(-j),
                )
                go(("rz", q, p), copy, copy)

    def along_y(k):
        def copy(d):
            return rc(
                ysend.at[k, ymod(d)], yland.at[k, d - 1], ry_s.at[k, d - 1], ry_r.at[k, d - 1],
                dev(c, ymod(d), zh, me),
            )
        for d in YORD:
            go(("ry", k, d), copy(d), copy(d))

    def near_sum():
        for q in (0, 1):
            for p in range(4):
                got(("rz", q, p))
        acc0[...] += zland[0].astype(F32) + zland[1].astype(F32)
        ysend[0] = acc0[...].astype(BF16)
        along_y(0)

    def far_sum():
        ysend[1] = (lgf[2, :, c] + lgr[2].astype(F32)).astype(BF16)
        along_y(1)

    def far_end():
        t = lgf[2, y, c] + lgr[2, y].astype(F32)
        for d in YORD[::-1]:
            got(("ry", 1, d))
            t = t + yland[1, d - 1].astype(F32)
        fsend[...] = t.astype(BF16)
        copy = rc(fsend, fland, rf_s, rf_r, zdev(2))
        go(("rf",), copy, copy)

    def near_end():
        t = acc0[y]
        for d in YORD[::-1]:
            got(("ry", 0, d))
            t = t + yland[0, d - 1].astype(F32)
        pg_out[...] = t

    def end():
        got(("rf",))
        pg_out[...] = (pg_out[...] + fland[...].astype(F32)) * (1.0 / math.sqrt(256 * 64))
        drain()

    def backward(r0, r1):
        @pl.loop(r0, r1)
        def _(r):
            at = pl.ds(pl.multiple_of(r * 32, 32), 32)
            g = gate[at, :].astype(F32)
            u = up[at, :].astype(F32)
            hg = hgrad[at, :]
            sig = jax.nn.sigmoid(g)
            gu_out[at, :] = (hg * g * sig).astype(BF16)
            gg_out[at, :] = (hg * u * sig * (1.0 + g * (1.0 - sig))).astype(BF16)

    copy_z(1)
    copy_z(3)
    first(0)
    make_hidden()
    unit(1, 0)
    got(("wz", 1))
    first(1)
    relay_z(0)
    got(("wz", 3))
    relay_z(1)
    first(3)
    stage_a(0)
    unit(2, 0)
    unit(1, 1)
    stage_a(1)
    loads[5].wait()
    unit(1, 3)
    stage_b(0)
    unit(3, 0)
    got(("wz2", 0))
    got(("wz2", 1))
    first(2)
    stage_a(2)
    unit(2, 1)
    stage_b(1)
    unit(2, 3)
    unit(4, 0)
    unit(1, 2)
    stage_a(3)
    stage_b(2)
    unit(3, 1)
    stage_c(0)
    stage_h(0)
    unit(3, 3)
    stage_a(4)
    unit(2, 2)
    stage_c(1)
    stage_h(1)
    unit(4, 1)
    stage_b(3)
    stage_a(5)
    unit(4, 3)
    unit(3, 2)
    stage_b(4)
    stage_c(2)
    stage_h(2)
    stage_a(6)
    paired(0)
    paired(1)
    unit(4, 2)
    stage_c(3)
    stage_h(3)
    stage_b(5)
    stage_a(7)
    paired(2)
    stage_c(4)
    stage_h(4)
    stage_b(6)
    paired(3)
    stage_c(5)
    stage_h(5)
    stage_b(7)
    paired(4)
    stage_c(6)
    paired(5)
    stage_c(7)
    paired(6)
    paired(7)
    far_sum()
    stage_h(6)
    stage_h(7)
    near_sum()
    backward(0, 8)
    far_end()
    near_end()
    end()


def finish(a, b, c, d, oa, ob, oc, od):
    for x, o in ((a, oa), (b, ob), (c, oc), (d, od)):
        o[...] = x[...]


def per_device(teacher, projector, residual, gate_pre, up_pre, down_weight):
    vm = pl.BlockSpec(memory_space=pltpu.VMEM)
    hbm = pl.BlockSpec(memory_space=pl.ANY)
    dma = pltpu.SemaphoreType.DMA
    outs = (
        jax.ShapeDtypeStruct((32, 384), F32),
        jax.ShapeDtypeStruct((32, 2048), BF16),
        jax.ShapeDtypeStruct((256, 1024), BF16),
        jax.ShapeDtypeStruct((256, 1024), BF16),
    )
    results = pl.pallas_call(
        kernel,
        out_shape=outs,
        in_specs=[hbm] * 6,
        out_specs=(vm,) * 4,
        scratch_shapes=[
            pltpu.VMEM((256, 384), BF16),
            pltpu.VMEM((32, 2048), BF16),
            pltpu.VMEM((256, 1024), BF16),
            pltpu.VMEM((256, 1024), BF16),
            pltpu.VMEM((4, 8, 2, 32, 1408), BF16),
            pltpu.VMEM((256, 1408), BF16),
            pltpu.VMEM((NC, 256, WIDE), BF16),
            pltpu.VMEM((NC, 7, 32, WIDE), BF16),
            pltpu.VMEM((NC, 256, WIDE), BF16),
            pltpu.VMEM((256, 1024), F32),
            pltpu.VMEM((4, 8, 2, 32, 384), F32),
            pltpu.VMEM((4, 8, 2, 32, 384), BF16),
            pltpu.VMEM((4, 8, 32, 384), BF16),
            pltpu.VMEM((8, 32, 384), F32),
            pltpu.VMEM((2, 8, 32, 384), BF16),
            pltpu.VMEM((2, 7, 32, 384), BF16),
            pltpu.VMEM((2, 8, 32, 384), BF16),
            pltpu.VMEM((2, 8, 32, 384), BF16),
            pltpu.VMEM((32, 384), BF16),
            pltpu.VMEM((32, 384), BF16),
            dma((6,)), dma((4,)), dma((4,)),
            dma((2, 4, 4)), dma((2, 4, 4)), dma((2, 5, 4)), dma((2, 5, 4)),
            dma((NC, 7)), dma((NC, 7)), dma((NC, 7)), dma((NC, 7)),
            dma((4, 4)), dma((4, 4)), dma((2, 7)), dma((2, 7)), dma((2, 4)), dma((2, 4)), dma(()), dma(()),
        ],
        compiler_params=pltpu.CompilerParams(
            collective_id=0, has_side_effects=True, vmem_limit_bytes=56 * 1024 * 1024
        ),
        cost_estimate=pl.CostEstimate(flops=2950000000, bytes_accessed=4000000, transcendentals=524288),
    )(down_weight.T, projector.T, teacher, residual, gate_pre, up_pre)
    pg, gr, gg, gu = pl.pallas_call(
        finish,
        out_shape=outs,
        in_specs=[vm] * 4,
        out_specs=(vm,) * 4,
    )(*results)
    return pg.T, gr, gg, gu


def solution(mesh):
    in_specs = (
        P("dp", "tensor"),
        P("tensor", "dp"),
        P(("dp", "tensor"), None),
        P("dp", "tensor"),
        P("dp", "tensor"),
        P("tensor", "dp"),
    )
    out_specs = (P("tensor", "dp"), P(("dp", "tensor"), None), P("dp", "tensor"), P("dp", "tensor"))
    return jax.shard_map(
        per_device, mesh=mesh, in_specs=in_specs, out_specs=out_specs, check_vma=False
    )
```

time: 418 us -> 87.1 us (0.21)
  waiting for transfers between devices: 363 us -> 0 us
  Pallas kernels: 0 us -> 86.3 us
  blocking collectives: 19 us -> 0 us
  matrix products: 14.4 us -> 0 us
  between operations: 13.8 us -> 0.64 us
    all_gather x3 -> x0, waiting for transfers between devices: 213 us -> none  [the longest x1 97 us: per_device(): down_whole = lax.all_gather(down_weight, 'dp', axis=1, tiled=True)]
    reduce_scatter x1 -> x0, waiting for transfers between devices: 148 us -> none  [per_device(): lax.psum_scatter(local_grad, 'dp', scatter_dimension=1, tiled=True)]
    pallas_call x0 -> x2, Pallas kernels: none -> 86.3 us  [the longest x1 84 us: per_device(): pl.pallas_call(kernel, out_shape=outs, in_specs=[hbm] * 6, out_specs=(vm,...]
    all_to_all x1 -> x0, blocking collectives: 19 us -> none  [per_device(): lax.all_to_all(stacked, 'tensor', split_axis=0, concat_axis=0, tiled=True)]
    dot_general x4 -> x0, matrix products: 14.4 us -> none  [the longest x1 4.71 us: per_device(): lax.dot_general(grad_rows, down_whole, contract_cols, preferred_element_t...]
  transfers between devices with their start and end apart: 4 -> 0, of which waited for: 4 -> 0; matrix products, arithmetic and copies ran while one was open for 2% -> 0% of each run, Pallas kernels for 0% -> 0%
where the time goes in v2:
time: 87.1 us; the launch traced here: 87 us
  Pallas kernels  86.3 us (99%)
    pallas_call x1, Pallas kernels, per_device(): pl.pallas_call(kernel, out_shape=outs, in_specs=[hbm] * 6, out_specs=(vm,...  84 us
    pallas_call x1, Pallas kernels, per_device(): pl.pallas_call(finish, out_shape=outs, in_specs=[vm] * 4, out_specs=(vm,)...  2.34 us

profile of v2, /device:TPU:1, one launch (start us, length us, event | category | flops | bytes accessed | tf_op | source)
XLA Modules:
  0.0 87.0 jit_solution(12977656050488303065)
XLA Ops:
  0.6 84.0 %shard_map.93 = (f32[32,384]{1,0:T(8,128)}, bf16[32,2048]{1,0:T(8,128)(2,1)}, bf16[256,1024]{1,0:T(8,128)(2,1)}, bf16[256,1024]{1,0:T(8,128)(2,1)}) custom-call(bf16[32,1024]{1,0:T(8,128)(2,1)} %bitcast.3, bf16[32,384]{1,0:T(8,128)(2,1)} %bitcast.5, bf16[256,384]{1,0:T(8,128)(2,1)} %teacher_in.1, bf16[32,2048]{1,0:T(8,128)(2,1)} %residual_in.1, ...), custom_call_target="tpu_custom_call" | custom-call | flops 2950000128 | bytes 4000000 | tf_op jit(solution)/shard_map/pallas_call | solution.py:398
  84.6 2.3 %shard_map.94 = (f32[32,384]{1,0:T(8,128)}, bf16[32,2048]{1,0:T(8,128)(2,1)}, bf16[256,1024]{1,0:T(8,128)(2,1)}, bf16[256,1024]{1,0:T(8,128)(2,1)}) custom-call(f32[32,384]{1,0:T(8,128)} %get-tuple-element.12.a, bf16[32,2048]{1,0:T(8,128)(2,1)} %get-tuple-element.13.b, bf16[256,1024]{1,0:T(8,128)(2,1)} %get-tuple-element.14.c, ...), custom_call_target="tpu_custom_call" | custom-call | tf_op jit(solution)/shard_map/pallas_call | solution.py:434

commit v3 on v2

--- a/solution.py
+++ b/solution.py
@@ -358,17 +358,17 @@
     stage_a(7)
     paired(2)
     stage_c(4)
-    stage_h(4)
     stage_b(6)
     paired(3)
+    stage_b(7)
+    stage_h(4)
     stage_c(5)
+    paired(4)
     stage_h(5)
-    stage_b(7)
-    paired(4)
     stage_c(6)
     paired(5)
+    paired(6)
     stage_c(7)
-    paired(6)
     paired(7)
     far_sum()
     stage_h(6)

time: 87.1 us -> 86.3 us (level)
  no operation moved by 1% of the time
where the time goes in v3:
time: 86.3 us; the launch traced here: 86.1 us
  Pallas kernels  85.5 us (99%)
    pallas_call x1, Pallas kernels, per_device(): pl.pallas_call(kernel, out_shape=outs, in_specs=[hbm] * 6, out_specs=(vm,...  83.1 us
    pallas_call x1, Pallas kernels, per_device(): pl.pallas_call(finish, out_shape=outs, in_specs=[vm] * 4, out_specs=(vm,)...  2.34 us

profile of v3, /device:TPU:1, one launch (start us, length us, event | category | flops | bytes accessed | tf_op | source)
XLA Modules:
  0.0 86.1 jit_solution(11583552650067817611)
XLA Ops:
  0.6 83.1 %shard_map.93 = (f32[32,384]{1,0:T(8,128)}, bf16[32,2048]{1,0:T(8,128)(2,1)}, bf16[256,1024]{1,0:T(8,128)(2,1)}, bf16[256,1024]{1,0:T(8,128)(2,1)}) custom-call(bf16[32,1024]{1,0:T(8,128)(2,1)} %bitcast.3, bf16[32,384]{1,0:T(8,128)(2,1)} %bitcast.5, bf16[256,384]{1,0:T(8,128)(2,1)} %teacher_in.1, bf16[32,2048]{1,0:T(8,128)(2,1)} %residual_in.1, ...), custom_call_target="tpu_custom_call" | custom-call | flops 2950000128 | bytes 4000000 | tf_op jit(solution)/shard_map/pallas_call | solution.py:398
  83.8 2.3 %shard_map.94 = (f32[32,384]{1,0:T(8,128)}, bf16[32,2048]{1,0:T(8,128)(2,1)}, bf16[256,1024]{1,0:T(8,128)(2,1)}, bf16[256,1024]{1,0:T(8,128)(2,1)}) custom-call(f32[32,384]{1,0:T(8,128)} %get-tuple-element.12.a, bf16[32,2048]{1,0:T(8,128)(2,1)} %get-tuple-element.13.b, bf16[256,1024]{1,0:T(8,128)(2,1)} %get-tuple-element.14.c, ...), custom_call_target="tpu_custom_call" | custom-call | tf_op jit(solution)/shard_map/pallas_call | solution.py:434
